TPU v7x, 512 devices: a whole 4x4x16 slice. The times are simulated.
512 devices in a mesh: blk: 128 (over y, z_lo, x), feat: 4 (over z_hi, core).
Axes of the slice: x: 4, y: 4, z: 16 (z_hi: 2, z_lo: 8; z = z_hi * 8 + z_lo), core: 2. Of those that a mesh axis runs over, the one named last changes fastest.
Arguments:
- features: bfloat16 [131072, 512], P('blk', 'feat')
- hop_noise: bfloat16 [2, 131072, 512], P(None, 'blk', 'feat'), may hold values from -4 to 4
- encoder_weight: bfloat16 [2, 512, 512], replicated, may hold values from -0.03125 to 0.03125
- block_target: int32 [128, 40], P('blk'), may hold values from 0 to 7
- block_source: int32 [128, 40], P('blk'), may hold values from 0 to 39
- block_count: int32 [128], P('blk'), may hold values from 10 to 40
- tile_mask: int32 [128, 40, 128, 128], P('blk'), may hold values 0 or 1
Outputs:
- encoded_one: bfloat16 [131072, 512], P('blk', 'feat')
- encoded_two: bfloat16 [131072, 512], P('blk', 'feat')
Inputs may be any that keep to these rules, and one draw needn't show every extreme that they name: Entries k < block_count of a partition's list are live, the others are ignored. `block_source`: window index: source partition offset index // 8 - 2, row block index % 8.
All inputs are finite; a program needn't handle non-finite values. No bound on the sum of `tile_mask` on one device may be relied on, other than what follows from the above.
Results may differ from a plain program's by a relative error of at most 0.015.
Values may be sent and summed in bfloat16 or wider, within the bound.
A program may use at most 64 MiB of HBM per device.

v0:
```python
import jax
import jax.numpy as jnp
from jax import lax
from jax.sharding import PartitionSpec as P

TILE = 128
TILES = 8
HALF = 2
K = 40
HOPS = 2


def passed_along(x, axis, by):
    size = lax.axis_size(axis)
    return lax.ppermute(x, axis, [(i, (i + by) % size) for i in range(size)])


def band_window(clipped):
    above = []
    moving = clipped
    for offset in range(HALF):
        moving = passed_along(moving, "blk", -1)
        above.append(moving)
    below = []
    moving = clipped
    for offset in range(HALF):
        moving = passed_along(moving, "blk", 1)
        below.append(moving)
    return below[::-1] + [clipped] + above


def encode_rows(noisy, weight, columns):
    my_first = lax.axis_index("feat") * columns
    my_columns = lax.dynamic_slice_in_dim(weight, my_first, columns, 1)
    summed = jnp.dot(
        lax.all_gather(noisy, "feat", axis=1, tiled=True),
        my_columns,
        preferred_element_type=jnp.float32,
    )
    return summed.astype(jnp.bfloat16)


def per_device(
    features, hop_noise, encoder_weight, block_target, block_source, block_count, tile_mask
):
    row_count = features.shape[0]
    columns = features.shape[1]
    mask_values = tile_mask[0].astype(jnp.bfloat16)
    targets = block_target[0]
    sources = block_source[0]
    active = jnp.arange(K) < block_count[0]
    routing = ((targets[:, None] == jnp.arange(TILES)[None, :]) & active[:, None]).astype(
        jnp.float32
    )
    current = features
    results = []
    for hop_index in range(HOPS):
        widened = current.astype(jnp.float32)
        squares = lax.psum(jnp.sum(widened * widened, axis=1), "feat")
        clipped = (widened / jnp.maximum(1.0, jnp.sqrt(squares))[:, None]).astype(jnp.bfloat16)
        window_tiles = jnp.concatenate(band_window(clipped), axis=0).reshape(-1, TILE, columns)
        picked = window_tiles[sources]
        products = jnp.einsum(
            "kij,kjf->kif", mask_values, picked, preferred_element_type=jnp.float32
        )
        aggregate = jnp.einsum("kt,kif->tif", routing, products).reshape(row_count, columns)
        noisy = (aggregate + hop_noise[hop_index].astype(jnp.float32)).astype(jnp.bfloat16)
        encoded = encode_rows(noisy, encoder_weight[hop_index], columns)
        results.append(encoded)
        current = encoded
    return (results[0], results[1])


def solution(mesh):
    in_specs = (
        P("blk", "feat"),
        P(None, "blk", "feat"),
        P(),
        P("blk", None),
        P("blk", None),
        P("blk"),
        P("blk", None, None, None),
    )
    out_specs = (P("blk", "feat"), P("blk", "feat"))
    return jax.shard_map(
        per_device, mesh=mesh, in_specs=in_specs, out_specs=out_specs, check_vma=False
    )
```

profile of v0, /device:TPU:1, one launch (start us, length us, event | category | flops | bytes accessed | tf_op | source)
XLA Modules:
  0.0 276.7 jit_solution(6634274752078948736)
XLA Ops:
  7.2 0.0 all-gather.3.cloned.1.call-start
  7.2 1.2 fusion.10
  8.4 20.6 %psum.14 = f32[1024]{0:T(1024)S(1)} all-reduce(f32[1024]{0:T(1024)S(1)} %fusion.10), channel_id=1, replica_groups=mesh['blk'=128,'feat'=4] {'feat'}, use_global_device_ids=true, to_apply=%region_1.0 | all-reduce | flops 1024 | bytes 8192 | tf_op jit(solution)/shard_map/psum | solution.py:59
  29.0 1.2 fusion.11
  30.2 1.9 collective-permute-start
  32.1 14.2 %collective-permute-start.2 = (bf16[1024,128]{1,0:T(8,128)(2,1)S(1)}, bf16[1024,128]{1,0:T(8,128)(2,1)S(1)}, u32[]{:S(2)}, u32[]{:S(2)}) collective-permute-start(bf16[1024,128]{1,0:T(8,128)(2,1)S(1)} %fusion.11), channel_id=1, source_target_pairs={{0,508},{4,0},{8,4},{12,8},{16,12},{20,16},{24,20},{28,24},{32,28}... | collective-permute-start | bytes 786440 | tf_op jit(solution)/shard_map/ppermute | solution.py:15
  46.3 1.8 collective-permute-done
  48.2 1.9 collective-permute-start.1
  50.1 0.7 fusion.28
  51.4 14.2 %collective-permute-start.3 = (bf16[1024,128]{1,0:T(8,128)(2,1)S(1)}, bf16[1024,128]{1,0:T(8,128)(2,1)S(1)}, u32[]{:S(2)}, u32[]{:S(2)}) collective-permute-start(bf16[1024,128]{1,0:T(8,128)(2,1)S(1)} %collective-permute-done.2), channel_id=1, source_target_pairs={{0,508},{4,0},{8,4},{12,8},{16,12},{20,16},{24,20},{28,24},{32,28}... | collective-permute-start | bytes 786440 | tf_op jit(solution)/shard_map/ppermute | solution.py:15
  65.6 0.5 collective-permute-done.1
  66.2 0.3 constant_dynamic-update-slice_fusion.2
  66.5 2.4 collective-permute-done.3
  69.0 1.0 copy-done.2
  70.0 3.3 %gather_fusion = bf16[40,128,128]{2,1,0:T(8,128)(2,1)} fusion(bf16[40,128,128]{2,1,0:T(8,128)(2,1)} %bitcast.46, s32[1024]{0:T(1024)S(1)} %pad_clamp_fusion), kind=kCustom, calls=%fused_computation | custom fusion | bytes 2621600 | tf_op jit(solution)/shard_map/gather | solution.py:62
  73.4 3.4 %fusion.6 = bf16[40,128,128]{2,1,0:T(8,128)(2,1)} fusion(bf16[40,128,128]{2,1,0:T(8,128)(2,1)} %gather_fusion, s32[1,40,128,128]{3,2,1,0:T(8,128)S(1)} %copy-done), kind=kOutput, calls=%fused_computation.8 | convolution fusion | flops 168427520 | bytes 5242880 | tf_op jit(solution)/shard_map/kij,kjf->kif/dot_general | solution.py:63
  76.8 2.7 copy.11
  79.5 1.7 fusion.2
  81.3 0.1 copy.9
  81.4 0.8 fusion.15
  82.1 0.0 all-gather.3.cloned.1.call-update
  82.2 0.0 all-gather.5.cloned.1.call-start
  82.2 2.1 fusion.31
  84.3 61.0 %all-gather.3.cloned.1.call-done = bf16[1024,512]{1,0:T(8,128)(2,1)} async-done(((bf16[1024,128]{1,0:T(8,128)(2,1)}), bf16[1024,512]{1,0:T(8,128)(2,1)}) %all-gather.3.cloned.1.call-update) | async-done | bytes 1048592 | tf_op jit(solution)/shard_map/all_gather | solution.py:36
  145.3 1.7 fusion.12
  147.1 14.0 %psum.15 = f32[1024]{0:T(1024)S(1)} all-reduce(f32[1024]{0:T(1024)S(1)} %get-tuple-element.4), channel_id=1, replica_groups=mesh['blk'=128,'feat'=4] {'feat'}, use_global_device_ids=true, to_apply=%region_3.0 | all-reduce | flops 1024 | bytes 8192 | tf_op jit(solution)/shard_map/psum | solution.py:59
  161.1 0.2 fusion.13
  161.3 3.1 %collective-permute-start.4 = (bf16[1024,128]{1,0:T(8,128)(2,1)S(1)}, bf16[1024,128]{1,0:T(8,128)(2,1)S(1)}, u32[]{:S(2)}, u32[]{:S(2)}) collective-permute-start(bf16[1024,128]{1,0:T(8,128)(2,1)S(1)} %fusion.13), channel_id=1, source_target_pairs={{0,4},{4,8},{8,12},{12,16},{16,20},{20,24},{24,28},{28,32},{32,36}... | collective-permute-start | bytes 786440 | tf_op jit(solution)/shard_map/ppermute | solution.py:15
  164.4 13.0 %collective-permute-start.6 = (bf16[1024,128]{1,0:T(8,128)(2,1)S(1)}, bf16[1024,128]{1,0:T(8,128)(2,1)S(1)}, u32[]{:S(2)}, u32[]{:S(2)}) collective-permute-start(bf16[1024,128]{1,0:T(8,128)(2,1)S(1)} %fusion.13), channel_id=1, source_target_pairs={{0,508},{4,0},{8,4},{12,8},{16,12},{20,16},{24,20},{28,24},{32,28}... | collective-permute-start | bytes 786440 | tf_op jit(solution)/shard_map/ppermute | solution.py:15
  177.4 3.5 %collective-permute-done.4 = bf16[1024,128]{1,0:T(8,128)(2,1)S(1)} collective-permute-done((bf16[1024,128]{1,0:T(8,128)(2,1)S(1)}, bf16[1024,128]{1,0:T(8,128)(2,1)S(1)}, u32[]{:S(2)}, u32[]{:S(2)}) %collective-permute-start.4) | collective-permute-done | bytes 262176 | tf_op jit(solution)/shard_map/ppermute | solution.py:15
  180.9 1.9 collective-permute-start.5
  182.9 14.2 %collective-permute-start.7 = (bf16[1024,128]{1,0:T(8,128)(2,1)S(1)}, bf16[1024,128]{1,0:T(8,128)(2,1)S(1)}, u32[]{:S(2)}, u32[]{:S(2)}) collective-permute-start(bf16[1024,128]{1,0:T(8,128)(2,1)S(1)} %collective-permute-done.6), channel_id=1, source_target_pairs={{0,508},{4,0},{8,4},{12,8},{16,12},{20,16},{24,20},{28,24},{32,28}... | collective-permute-start | bytes 786440 | tf_op jit(solution)/shard_map/ppermute | solution.py:15
  197.1 2.6 collective-permute-done.5
  199.7 0.7 constant_dynamic-update-slice_fusion.9
  200.4 0.7 constant_dynamic-update-slice_fusion.8
  201.1 0.9 constant_dynamic-update-slice_fusion.7
  202.0 0.7 constant_dynamic-update-slice_fusion.6
  202.7 0.7 constant_dynamic-update-slice_fusion.5
  203.4 3.2 %gather_fusion.1 = bf16[40,128,128]{2,1,0:T(8,128)(2,1)} fusion(bf16[40,128,128]{2,1,0:T(8,128)(2,1)} %bitcast.11, s32[1024]{0:T(1024)S(1)} %pad_clamp_fusion), kind=kCustom, calls=%fused_computation.1 | custom fusion | bytes 2621600 | tf_op jit(solution)/shard_map/gather | solution.py:62
  206.6 3.4 %fusion.4 = bf16[40,128,128]{2,1,0:T(8,128)(2,1)} fusion(bf16[40,128,128]{2,1,0:T(8,128)(2,1)} %gather_fusion.1, s32[1,40,128,128]{3,2,1,0:T(8,128)S(1)} %copy-done), kind=kOutput, calls=%fused_computation.6 | convolution fusion | flops 168427520 | bytes 5242880 | tf_op jit(solution)/shard_map/kij,kjf->kif/dot_general | solution.py:63
  210.1 2.1 copy.12
  212.2 0.3 fusion
  212.6 0.1 copy.10
  212.7 0.6 copy-done.5
  213.3 0.8 fusion.14
  214.0 0.0 all-gather.5.cloned.1.call-update
  214.1 53.4 %all-gather.5.cloned.1.call-done = bf16[1024,512]{1,0:T(8,128)(2,1)} async-done(((bf16[1024,128]{1,0:T(8,128)(2,1)}), bf16[1024,512]{1,0:T(8,128)(2,1)}) %all-gather.5.cloned.1.call-update) | async-done | bytes 1048592 | tf_op jit(solution)/shard_map/all_gather | solution.py:36
  267.4 2.4 convolution_convert_fusion
  (23 shorter events, 0.2 us)
Async XLA Ops:
  7.2 59.0 %copy-start.1 = (bf16[1024,128]{1,0:T(8,128)(2,1)S(1)}, bf16[1024,128]{1,0:T(8,128)(2,1)}, u32[]{:S(2)}) copy-start(bf16[1024,128]{1,0:T(8,128)(2,1)} %param.7) | copy-start | bytes 786436
  7.2 138.1 %all-gather.3.cloned.1.call-start = ((), (), s32[]{:S(2)}) async-start(), calls=%async_computation | async-start | bytes 1310720 | tf_op jit(solution)/shard_map/all_gather | solution.py:36
  30.2 17.9 %collective-permute-start = (bf16[1024,128]{1,0:T(8,128)(2,1)S(1)}, bf16[1024,128]{1,0:T(8,128)(2,1)S(1)}, u32[]{:S(2)}, u32[]{:S(2)}) collective-permute-start(bf16[1024,128]{1,0:T(8,128)(2,1)S(1)} %fusion.11), channel_id=1, source_target_pairs={{0,4},{4,8},{8,12},{12,16},{16,20},{20,24},{24,28},{28,32},{32,36}... | collective-permute-start | bytes 786440 | tf_op jit(solution)/shard_map/ppermute | solution.py:15
  32.1 19.3 %collective-permute-start.2 = (bf16[1024,128]{1,0:T(8,128)(2,1)S(1)}, bf16[1024,128]{1,0:T(8,128)(2,1)S(1)}, u32[]{:S(2)}, u32[]{:S(2)}) collective-permute-start(bf16[1024,128]{1,0:T(8,128)(2,1)S(1)} %fusion.11), channel_id=1, source_target_pairs={{0,508},{4,0},{8,4},{12,8},{16,12},{20,16},{24,20},{28,24},{32,28}... | collective-permute-start | bytes 786440 | tf_op jit(solution)/shard_map/ppermute | solution.py:15
  48.2 17.9 %collective-permute-start.1 = (bf16[1024,128]{1,0:T(8,128)(2,1)S(1)}, bf16[1024,128]{1,0:T(8,128)(2,1)S(1)}, u32[]{:S(2)}, u32[]{:S(2)}) collective-permute-start(bf16[1024,128]{1,0:T(8,128)(2,1)S(1)} %collective-permute-done), channel_id=1, source_target_pairs={{0,4},{4,8},{8,12},{12,16},{16,20},{20,24},{24,28},{28,32},{32,36}... | collective-permute-start | bytes 786440 | tf_op jit(solution)/shard_map/ppermute | solution.py:15
  51.4 17.5 %collective-permute-start.3 = (bf16[1024,128]{1,0:T(8,128)(2,1)S(1)}, bf16[1024,128]{1,0:T(8,128)(2,1)S(1)}, u32[]{:S(2)}, u32[]{:S(2)}) collective-permute-start(bf16[1024,128]{1,0:T(8,128)(2,1)S(1)} %collective-permute-done.2), channel_id=1, source_target_pairs={{0,508},{4,0},{8,4},{12,8},{16,12},{20,16},{24,20},{28,24},{32,28}... | collective-permute-start | bytes 786440 | tf_op jit(solution)/shard_map/ppermute | solution.py:15
  68.9 1.1 copy-start.2
  70.0 3.4 %copy-start = (s32[1,40,128,128]{3,2,1,0:T(8,128)S(1)}, s32[1,40,128,128]{3,2,1,0:T(8,128)}, u32[]{:S(2)}) copy-start(s32[1,40,128,128]{3,2,1,0:T(8,128)} %param.13) | copy-start | bytes 7864324
  76.8 2.8 copy-start.6
  79.5 1.8 copy-start.4
  82.2 185.3 %all-gather.5.cloned.1.call-start = ((), (), s32[]{:S(2)}) async-start(), calls=%async_computation.1 | async-start | bytes 1310720 | tf_op jit(solution)/shard_map/all_gather | solution.py:36
  147.0 55.7 %copy-start.3 = (bf16[1024,128]{1,0:T(8,128)(2,1)}, bf16[1024,128]{1,0:T(8,128)(2,1)S(1)}, u32[]{:S(2)}) copy-start(bf16[1024,128]{1,0:T(8,128)(2,1)S(1)} %get-tuple-element.5) | copy-start | bytes 786436
  161.3 19.6 %collective-permute-start.4 = (bf16[1024,128]{1,0:T(8,128)(2,1)S(1)}, bf16[1024,128]{1,0:T(8,128)(2,1)S(1)}, u32[]{:S(2)}, u32[]{:S(2)}) collective-permute-start(bf16[1024,128]{1,0:T(8,128)(2,1)S(1)} %fusion.13), channel_id=1, source_target_pairs={{0,4},{4,8},{8,12},{12,16},{16,20},{20,24},{24,28},{28,32},{32,36}... | collective-permute-start | bytes 786440 | tf_op jit(solution)/shard_map/ppermute | solution.py:15
  164.4 18.4 %collective-permute-start.6 = (bf16[1024,128]{1,0:T(8,128)(2,1)S(1)}, bf16[1024,128]{1,0:T(8,128)(2,1)S(1)}, u32[]{:S(2)}, u32[]{:S(2)}) collective-permute-start(bf16[1024,128]{1,0:T(8,128)(2,1)S(1)} %fusion.13), channel_id=1, source_target_pairs={{0,508},{4,0},{8,4},{12,8},{16,12},{20,16},{24,20},{28,24},{32,28}... | collective-permute-start | bytes 786440 | tf_op jit(solution)/shard_map/ppermute | solution.py:15
  180.9 18.7 %collective-permute-start.5 = (bf16[1024,128]{1,0:T(8,128)(2,1)S(1)}, bf16[1024,128]{1,0:T(8,128)(2,1)S(1)}, u32[]{:S(2)}, u32[]{:S(2)}) collective-permute-start(bf16[1024,128]{1,0:T(8,128)(2,1)S(1)} %collective-permute-done.4), channel_id=1, source_target_pairs={{0,4},{4,8},{8,12},{12,16},{16,20},{20,24},{24,28},{28,32},{32,36}... | collective-permute-start | bytes 786440 | tf_op jit(solution)/shard_map/ppermute | solution.py:15
  182.9 19.9 %collective-permute-start.7 = (bf16[1024,128]{1,0:T(8,128)(2,1)S(1)}, bf16[1024,128]{1,0:T(8,128)(2,1)S(1)}, u32[]{:S(2)}, u32[]{:S(2)}) collective-permute-start(bf16[1024,128]{1,0:T(8,128)(2,1)S(1)} %collective-permute-done.6), channel_id=1, source_target_pairs={{0,508},{4,0},{8,4},{12,8},{16,12},{20,16},{24,20},{28,24},{32,28}... | collective-permute-start | bytes 786440 | tf_op jit(solution)/shard_map/ppermute | solution.py:15
  212.2 1.0 copy-start.5
Sparse Core Ops, SparseCore 0:
  82.3 62.9 all-gather.2
  214.2 53.2 all-gather.4
where the time goes:
time: 277 us
  waiting for transfers between devices  125 us (45%)
  starting transfers between devices  64.5 us (23%)
  blocking collectives  34.6 us (12%)
  local copies, waits for them, and re-layouts  18.3 us (7%)
  between operations  14.9 us (5%)
  matrix products  13 us (5%)
  other arithmetic  5.97 us (2%)
    all_gather x2, waiting for transfers between devices, encode_rows(): lax.all_gather(noisy, 'feat', axis=1, tiled=True)  114 us
    ppermute x8, starting transfers between devices, passed_along(): return lax.ppermute(x, axis, [(i, (i + by) % size) for i in range(size)])  64.4 us
    psum x2, blocking collectives, per_device(): squares = lax.psum(jnp.sum(widened * widened, axis=1), 'feat')  34.6 us
    ppermute x8, waiting for transfers between devices, passed_along(): return lax.ppermute(x, axis, [(i, (i + by) % size) for i in range(size)])  10.9 us
    dot_general x2, matrix products, per_device(): jnp.einsum('kij,kjf->kif', mask_values, picked, preferred_element_type=jn...  6.87 us
    gather x2, local copies, waits for them, and re-layouts, per_device(): picked = window_tiles[sources]  6.54 us
  transfers between devices with their start and end apart: 10, of which 7 were waited for; matrix products, arithmetic and copies ran while one was open for 2% of the time, Pallas kernels for 0%

commit v1 on v0

v1 whole, which is shorter than its diff:
```python
import jax
import jax.numpy as jnp
from jax import lax
from jax.experimental import pallas as pl
from jax.experimental.pallas import tpu as pltpu
from jax.sharding import PartitionSpec as P

TILE = 128
TILES = 8
K = 40
Q = 4
QB = TILES // Q
N_EARLY = 4
MESH = pl.DeviceIdType.MESH
F32 = jnp.float32
BF16 = jnp.bfloat16
SRC, KEEP, LAST, HAS = 40, 80, 120, 128


def remote(src, dst, sems, index, device):
    send, recv = sems
    return pltpu.make_async_remote_copy(
        src_ref=src,
        dst_ref=dst,
        send_sem=send.at[index],
        recv_sem=recv.at[index],
        device_id=device,
        device_id_type=MESH,
    )


def kernel(
    info, feat, noise, weight, mask, out_one, out_two,
    win0, win1, masks_in, masks, weights, noises, noisy, sums, squares, scales,
    encoded, own_one, own_two, noisy_two, others,
    halo0_s, halo0_r, halo1_s, halo1_r, z_s, z_r, core_s, core_r, fwd_s, fwd_r,
    noise_s, noise_r, sq_s, sq_r, sc_s, sc_r, swap_s, swap_r, local, out_sem,
):
    parts = lax.axis_size("blk")
    b = lax.axis_index("blk")
    f = lax.axis_index("feat")
    zh = lax.div(f, 2)
    core = lax.rem(f, 2)
    fz = lax.rem(f + 2, 4)
    fc = f + 1 - 2 * core
    fd = lax.rem(fc + 2, 4)
    nxt, prv = lax.rem(b + 1, parts), lax.rem(b + parts - 1, parts)
    nxt2, prv2 = lax.rem(b + 2, parts), lax.rem(b + parts - 2, parts)
    f_nxt = jnp.where(lax.rem(b, 32) == 31, fz, f)
    f_prv = jnp.where(lax.rem(b, 32) == 0, fz, f)

    def dev(blk, col):
        return {"blk": blk, "feat": col}

    halo0, halo1 = (halo0_s, halo0_r), (halo1_s, halo1_r)
    started = []

    def go(copy):
        copy.start()
        started.append(copy)

    loads = [
        pltpu.make_async_copy(feat, win0.at[pl.ds(16, 8)], local.at[0]),
        pltpu.make_async_copy(mask, masks_in, local.at[1]),
        pltpu.make_async_copy(noise.at[0], noises.at[2], local.at[2]),
        pltpu.make_async_copy(noise.at[1], noises.at[zh], local.at[3]),
        pltpu.make_async_copy(weight, weights, local.at[4]),
    ]
    for load in loads:
        load.start()

    barrier = pltpu.get_barrier_semaphore()
    for device in (
        dev(nxt, f), dev(prv, f), dev(nxt2, f), dev(prv2, f), dev(nxt, fz), dev(prv, fz),
        dev(b, fz), dev(b, fc), dev(b, fd),
    ):
        pl.semaphore_signal(barrier, inc=1, device_id=device, device_id_type=MESH)
    pl.semaphore_wait(barrier, 9)

    def halo0_copy(way, step, q):
        to = dev(nxt, f) if way == 0 else dev(prv, f)
        here = (16, 8, 0)[step] if way == 0 else (16, 24, 32)[step]
        there = (16, 8, 0)[step + 1] if way == 0 else (16, 24, 32)[step + 1]
        src = feat.at[pl.ds(q * QB, QB)] if step == 0 else win0.at[pl.ds(here + q * QB, QB)]
        return remote(src, win0.at[pl.ds(there + q * QB, QB)], halo0, (way * 2 + step) * Q + q, to)

    for q in range(Q):
        go(halo0_copy(0, 0, q))
        go(halo0_copy(1, 0, q))

    ones = jnp.ones((8, TILE), F32)
    for t in range(TILES):
        wide = feat[t].astype(F32)
        row = lax.dot_general(
            ones, wide * wide, (((1,), (1,)), ((), ())),
            precision=lax.Precision.HIGHEST, preferred_element_type=F32,
        )
        squares[0, t : t + 1, :] = row[0:1, :]
    for i, col in enumerate((fz, fc, fd)):
        go(remote(squares.at[0], squares.at[i + 1], (sq_s, sq_r), i, dev(b, col)))

    def noise_copy(t):
        return remote(noise.at[1, t], noises.at[zh, t], (noise_s, noise_r), t, dev(b, fz))

    for t in range(N_EARLY):
        go(noise_copy(t))

    def pass_on(q):
        for way in range(2):
            halo0_copy(way, 0, q).wait_recv()
            go(halo0_copy(way, 1, q))

    pass_on(0)
    pass_on(1)

    for i, col in enumerate((fz, fc, fd)):
        remote(squares.at[0], squares.at[i + 1], (sq_s, sq_r), i, dev(b, col)).wait_recv()
    total = (squares[0] + squares[1]) + (squares[2] + squares[3])
    scales[16:24, :] = 1.0 / jnp.maximum(1.0, jnp.sqrt(total))
    scale_copies = [
        remote(scales.at[pl.ds(16, 8)], scales.at[pl.ds(there, 8)], (sc_s, sc_r), i, dev(blk, f))
        for i, (there, blk) in enumerate(((8, nxt), (0, nxt2), (24, prv), (32, prv2)))
    ]
    for copy in scale_copies:
        go(copy)
    for q in range(2, Q):
        pass_on(q)

    loads[1].wait()

    def take_mask(k, carry):
        masks[k] = masks_in[info[k]].astype(F32).astype(BF16)
        return carry

    lax.fori_loop(0, K, take_mask, 0)
    loads[0].wait()
    for copy in scale_copies:
        copy.wait_recv()
    for q in range(Q):
        for way in range(2):
            halo0_copy(way, 1, q).wait_recv()

    def add_up(width, left, right):
        def step(i, acc):
            for u in range(4):
                k = i * 4 + u
                keep = info[KEEP + k].astype(F32)
                acc = acc * keep + jnp.dot(left(k), right(k), preferred_element_type=F32)
                sums[k, :, 0:width] = acc
            return acc

        lax.fori_loop(0, K // 4, step, jnp.zeros((TILE, width), F32))

    def scaled_mask(k):
        row = scales[pl.ds(info[SRC + k], 1), :]
        return (masks[k].astype(F32) * row).astype(BF16)

    add_up(TILE, scaled_mask, lambda k: win0[info[SRC + k]])

    def z_copy(t, col):
        return remote(noisy.at[col, t], noisy.at[col, t], (z_s, z_r), t, dev(b, fz))

    def core_copy(t, col):
        return remote(noisy.at[col, t], noisy.at[col, t], (core_s, core_r), t, dev(b, fc))

    def fwd_copy(t, col):
        return remote(noisy.at[col, t], noisy.at[col, t], (fwd_s, fwd_r), t, dev(b, fc))

    loads[2].wait()
    for t in range(TILES):
        has = info[HAS + t].astype(F32)
        rows = sums[info[LAST + t], :, 0:TILE] * has
        noisy[f, t] = (rows + noises[2, t].astype(F32)).astype(BF16)
        go(z_copy(t, f))
        go(core_copy(t, f))

    loads[4].wait()

    def halo1_copy(way, step, t):
        to = dev(nxt, f_nxt) if way == 0 else dev(prv, f_prv)
        here = (16, 8, 0)[step] if way == 0 else (16, 24, 32)[step]
        there = (16, 8, 0)[step + 1] if way == 0 else (16, 24, 32)[step + 1]
        return remote(win1.at[here + t], win1.at[there + t], halo1, (way * 2 + step) * TILES + t, to)

    outs = []

    def encode(t):
        core_copy(t, fc).wait_recv()
        fwd_copy(t, fd).wait_recv()
        left = jnp.concatenate([noisy[g, t] for g in range(4)], axis=1)
        rounded = jnp.dot(left, weights[0], preferred_element_type=F32).astype(BF16)
        wide = rounded.astype(F32)
        norm = jnp.sqrt(jnp.sum(wide * wide, axis=1, keepdims=True))
        inverse = 1.0 / jnp.maximum(1.0, norm)
        for g in range(4):
            encoded[g] = rounded[:, g * TILE : (g + 1) * TILE]
        own_one[t] = encoded[f]
        for half in range(2):
            win1[16 + t, half] = (encoded[half * 2 + core].astype(F32) * inverse).astype(BF16)
        for way in range(2):
            go(halo1_copy(way, 0, t))
        copy = pltpu.make_async_copy(own_one.at[t], out_one.at[t], out_sem.at[t])
        copy.start()
        outs.append(copy)

    def pass_on_one(t):
        for way in range(2):
            halo1_copy(way, 0, t).wait_recv()
            go(halo1_copy(way, 1, t))

    for t in range(TILES + 3):
        if t < TILES:
            z_copy(t, fz).wait_recv()
            go(fwd_copy(t, fz))
        if 0 <= t - 1 < TILES:
            encode(t - 1)
        if t == 5:
            for late in range(N_EARLY, TILES):
                go(noise_copy(late))
        if 0 <= t - 3 < TILES:
            pass_on_one(t - 3)

    for t in range(TILES):
        for way in range(2):
            halo1_copy(way, 1, t).wait_recv()

    add_up(
        2 * TILE,
        lambda k: masks[k],
        lambda k: jnp.concatenate([win1[info[SRC + k], 0], win1[info[SRC + k], 1]], axis=1),
    )

    def swap_copy(t):
        return remote(noisy_two.at[t], others.at[t], (swap_s, swap_r), t, dev(b, fc))

    loads[3].wait()
    for t in range(TILES):
        remote(
            noise.at[1, t], noises.at[1 - zh, t], (noise_s, noise_r), t, dev(b, fz)
        ).wait_recv()
        has = info[HAS + t].astype(F32)
        rows = sums[info[LAST + t]] * has
        for half in range(2):
            noisy_two[t, half] = (
                rows[:, half * TILE : (half + 1) * TILE] + noises[half, t].astype(F32)
            ).astype(BF16)
        go(swap_copy(t))

    mine = pl.ds(pl.multiple_of(f * TILE, TILE), TILE)
    upper = pl.multiple_of(core * TILE, TILE)
    other = pl.multiple_of(TILE - core * TILE, TILE)
    for t in range(TILES):
        swap_copy(t).wait_recv()
        left = jnp.concatenate(
            [noisy_two[t, 0], noisy_two[t, 1], others[t, 0], others[t, 1]], axis=1
        )
        right = jnp.concatenate(
            [
                weights[1, pl.ds(upper, TILE), mine],
                weights[1, pl.ds(upper + 2 * TILE, TILE), mine],
                weights[1, pl.ds(other, TILE), mine],
                weights[1, pl.ds(other + 2 * TILE, TILE), mine],
            ],
            axis=0,
        )
        own_two[t] = jnp.dot(left, right, preferred_element_type=F32).astype(BF16)
        copy = pltpu.make_async_copy(own_two.at[t], out_two.at[t], out_sem.at[TILES + t])
        copy.start()
        outs.append(copy)

    for copy in started:
        copy.wait_send()
    for copy in outs:
        copy.wait()


def list_order(targets, sources, count):
    spots = jnp.arange(K)
    live = spots < count
    key = jnp.where(live, targets, TILES) * 64 + spots
    rank = jnp.sum(key[None, :] < key[:, None], axis=1)
    at = rank[:, None] == spots[None, :]
    perm = jnp.sum(jnp.where(at, spots[:, None], 0), axis=0)
    src = jnp.sum(jnp.where(at, sources[:, None], 0), axis=0)
    low = jnp.sum(jnp.where(at, (key // 64)[:, None], 0), axis=0)
    keep = (jnp.concatenate([jnp.full((1,), -1, low.dtype), low[:-1]]) == low).astype(jnp.int32)
    tiles = jnp.arange(TILES)
    last = jnp.maximum(jnp.sum(key[None, :] < (tiles[:, None] + 1) * 64, axis=1) - 1, 0)
    has = jnp.any((key // 64)[None, :] == tiles[:, None], axis=1)
    return jnp.concatenate([v.astype(jnp.int32) for v in (perm, src, keep, last, has)])


def per_device(
    features, hop_noise, encoder_weight, block_target, block_source, block_count, tile_mask
):
    info = list_order(block_target[0], block_source[0], block_count[0])
    tiles = (TILES, TILE, TILE)
    dma = pltpu.SemaphoreType.DMA
    anywhere = pl.BlockSpec(memory_space=pl.ANY)
    one, two = pl.pallas_call(
        kernel,
        out_shape=[jax.ShapeDtypeStruct(tiles, BF16)] * 2,
        in_specs=[
            pl.BlockSpec(memory_space=pltpu.SMEM),
            pl.BlockSpec(memory_space=pltpu.VMEM),
            anywhere, anywhere, anywhere,
        ],
        out_specs=[anywhere, anywhere],
        scratch_shapes=[
            pltpu.VMEM((K, TILE, TILE), BF16),
            pltpu.VMEM((K, 2, TILE, TILE), BF16),
            pltpu.VMEM((K, TILE, TILE), jnp.int32),
            pltpu.VMEM((K, TILE, TILE), BF16),
            pltpu.VMEM((2, 512, 512), BF16),
            pltpu.VMEM((3,) + tiles, BF16),
            pltpu.VMEM((4,) + tiles, BF16),
            pltpu.VMEM((K, TILE, 2 * TILE), F32),
            pltpu.VMEM((4, TILES, TILE), F32),
            pltpu.VMEM((K, TILE), F32),
            pltpu.VMEM((4, TILE, TILE), BF16),
            pltpu.VMEM(tiles, BF16),
            pltpu.VMEM(tiles, BF16),
            pltpu.VMEM((TILES, 2, TILE, TILE), BF16),
            pltpu.VMEM((TILES, 2, TILE, TILE), BF16),
            dma((4 * Q,)), dma((4 * Q,)),
            dma((4 * TILES,)), dma((4 * TILES,)),
            dma((TILES,)), dma((TILES,)),
            dma((TILES,)), dma((TILES,)),
            dma((TILES,)), dma((TILES,)),
            dma((TILES,)), dma((TILES,)),
            dma((3,)), dma((3,)),
            dma((4,)), dma((4,)),
            dma((TILES,)), dma((TILES,)),
            dma((5,)),
            dma((2 * TILES,)),
        ],
        compiler_params=pltpu.CompilerParams(
            collective_id=0, has_side_effects=True, vmem_limit_bytes=40 << 20
        ),
    )(
        info,
        features.reshape(tiles),
        hop_noise.reshape((2,) + tiles),
        encoder_weight,
        tile_mask[0],
    )
    return one.reshape(features.shape), two.reshape(features.shape)


def solution(mesh):
    in_specs = (
        P("blk", "feat"),
        P(None, "blk", "feat"),
        P(),
        P("blk", None),
        P("blk", None),
        P("blk"),
        P("blk", None, None, None),
    )
    out_specs = (P("blk", "feat"), P("blk", "feat"))
    return jax.shard_map(
        per_device, mesh=mesh, in_specs=in_specs, out_specs=out_specs, check_vma=False
    )
```

time: 277 us -> 129 us (0.47)
  waiting for transfers between devices: 125 us -> 0 us
  Pallas kernels: 0 us -> 119 us
  starting transfers between devices: 64.5 us -> 0 us
  blocking collectives: 34.6 us -> 0 us
  between operations: 14.9 us -> 1.31 us
  matrix products: 13 us -> 0 us
  local copies, waits for them, and re-layouts: 18.3 us -> 6.44 us
  other arithmetic: 5.97 us -> 2.66 us
    pallas_call x0 -> x1, Pallas kernels: none -> 119 us  [per_device(): pl.pallas_call(kernel, out_shape=[jax.ShapeDtypeStruct(tiles, BF16)] * 2,...]
    all_gather x2 -> x0, waiting for transfers between devices: 114 us -> none  [encode_rows(): lax.all_gather(noisy, 'feat', axis=1, tiled=True)]
    ppermute x8 -> x0, starting transfers between devices: 64.4 us -> none  [passed_along(): return lax.ppermute(x, axis, [(i, (i + by) % size) for i in range(size)])]
    psum x2 -> x0, blocking collectives: 34.6 us -> none  [per_device(): squares = lax.psum(jnp.sum(widened * widened, axis=1), 'feat')]
    dot_general x6 -> x0, matrix products: 13 us -> none  [the longest x2 6.87 us: per_device(): jnp.einsum('kij,kjf->kif', mask_values, picked, preferred_element_type=jn...]
    ppermute x8 -> x0, waiting for transfers between devices: 10.9 us -> none  [passed_along(): return lax.ppermute(x, axis, [(i, (i + by) % size) for i in range(size)])]
    gather x2 -> x0, local copies, waits for them, and re-layouts: 6.54 us -> none  [per_device(): picked = window_tiles[sources]]
    dot_general x4 -> x0, local copies, waits for them, and re-layouts: 5.08 us -> none  [the longest x2 4.88 us: per_device(): jnp.einsum('kij,kjf->kif', mask_values, picked, preferred_element_type=jn...]
  transfers between devices with their start and end apart: 10 -> 0, of which waited for: 7 -> 0; matrix products, arithmetic and copies ran while one was open for 2% -> 0% of each run, Pallas kernels for 0% -> 0%
where the time goes in v1:
time: 129 us
  Pallas kernels  119 us (92%)
  local copies, waits for them, and re-layouts  6.44 us (5%)
  other arithmetic  2.66 us (2%)
  between operations  1.31 us (1%)
    pallas_call x1, Pallas kernels, per_device(): pl.pallas_call(kernel, out_shape=[jax.ShapeDtypeStruct(tiles, BF16)] * 2,...  119 us
    unnamed x10, local copies, waits for them, and re-layouts  6.36 us

profile of v1, /device:TPU:1, one launch (start us, length us, event | category | flops | bytes accessed | tf_op | source)
XLA Modules:
  0.0 129.1 jit_solution(18085506553329594018)
XLA Ops:
  1.3 0.7 and_select_fusion.1
  2.0 0.7 fusion.5
  2.6 0.2 convert_reduce_fusion.1
  2.8 0.2 convert_reduce_fusion
  3.0 0.1 fusion
  3.1 0.8 select_reduce_fusion
  3.9 0.1 compare_convert_fusion
  4.0 0.1 concatenate.7.info
  4.0 0.0 copy-start
  4.0 1.7 %copy-done = s32[1,40,128,128]{3,2,1,0:T(8,128)S(1)} copy-done((s32[1,40,128,128]{3,2,1,0:T(8,128)S(1)}, s32[1,40,128,128]{3,2,1,0:T(8,128)}, u32[]{:S(2)}) %copy-start) | copy-done | bytes 2621464
  5.8 0.0 copy-start.1
  5.8 1.2 copy-done.1
  7.0 0.0 copy-start.2
  7.0 1.0 copy-done.2
  8.0 0.0 copy-start.3
  8.0 0.9 copy-done.3
  9.0 118.7 %shard_map.86 = (bf16[8,128,128]{2,1,0:T(8,128)(2,1)S(1)}, bf16[8,128,128]{2,1,0:T(8,128)(2,1)S(1)}) custom-call(s32[136]{0:T(256)S(1)} %concatenate.7.info, bf16[8,128,128]{2,1,0:T(8,128)(2,1)S(1)} %bitcast.18, bf16[2,8,128,128]{3,2,1,0:T(8,128)(2,1)S(1)} %bitcast.17, bf16[2,512,512]{2,1,0:T(8,128)(2,1)S(1)} %copy-done.1, s32[40,128,128]{2,1,0:T(8,128)S(1)} %bitcast.16), custom_call_target="tpu_custom_call" | custom-call | tf_op jit(solution)/shard_map/pallas_call | solution.py:300
  127.7 0.7 copy.12
  128.4 0.7 copy.13
  (3 shorter events, 0.0 us)
Async XLA Ops:
  4.0 1.7 %copy-start = (s32[1,40,128,128]{3,2,1,0:T(8,128)S(1)}, s32[1,40,128,128]{3,2,1,0:T(8,128)}, u32[]{:S(2)}) copy-start(s32[1,40,128,128]{3,2,1,0:T(8,128)} %param.13) | copy-start | bytes 7864324
  5.8 1.2 copy-start.1
  7.0 1.0 copy-start.2
  8.0 0.9 copy-start.3

commit v2 on v1

v2 whole, which is shorter than its diff:
```python
import jax
import jax.numpy as jnp
from jax import lax
from jax.experimental import pallas as pl
from jax.experimental.pallas import tpu as pltpu
from jax.sharding import PartitionSpec as P

TILE = 128
TILES = 8
K = 40
Q = 4
QB = TILES // Q
EARLY = 3
LATE_AT = 7
WINDOW = 3
DRIP = 8
LAG = 2
MESH = pl.DeviceIdType.MESH
F32 = jnp.float32
BF16 = jnp.bfloat16
SRC, KEEP, LAST, HAS = 40, 80, 120, 128


class Links:
    def __init__(self, sems):
        self.sems = sems
        self.started = []
        self.known = {}
        self.arrived = set()

    def go(self, name, index, src, dst, device, lands=None, when=None):
        send, recv = self.sems[name]
        lands = index if lands is None else lands
        copy = pltpu.make_async_remote_copy(
            src_ref=src, dst_ref=dst, send_sem=send.at[index], recv_sem=recv.at[lands],
            device_id=device, device_id_type=MESH,
        )
        if when is None:
            copy.start()
        else:
            pl.when(when)(copy.start)
        self.started.append((copy, when, (name, index)))
        self.known[name, lands] = copy

    def sent(self, name, index):
        for i, (copy, when, at) in enumerate(self.started):
            if at == (name, index):
                copy.wait_send()
                del self.started[i]
                return

    def arrive(self, name, index):
        self.known[name, index].wait_recv()
        self.arrived.add((name, index))

    def finish(self):
        for copy, when, _ in self.started:
            if when is None:
                copy.wait_send()
            else:
                pl.when(when)(copy.wait_send)
        for at, copy in self.known.items():
            if at not in self.arrived:
                copy.wait_recv()


def kernel(
    info, feat, noise, weight, mask, out_one, out_two,
    win0, win1, masks_in, masks, weights, noises, noisy, sums, squares, chips, scales,
    encoded, own_one, own_two, noisy_two, others,
    halo0_s, halo0_r, halo1_s, halo1_r, z_s, z_r, core_s, core_r, fwd_s, fwd_r,
    noise_s, noise_r, sq_s, sq_r, sc_s, sc_r, swap_s, swap_r, local, out_sem,
):
    parts = lax.axis_size("blk")
    b = lax.axis_index("blk")
    f = lax.axis_index("feat")
    zh = lax.div(f, 2)
    core = lax.rem(f, 2)
    fz = lax.rem(f + 2, 4)
    fc = f + 1 - 2 * core
    fd = lax.rem(fc + 2, 4)
    row_at = lax.rem(b, 32)
    x = lax.rem(b, 4)
    inner = (x == 1) | (x == 2)
    low, high = x < 2, x >= 2

    def at(by):
        return lax.rem(b + by + parts, parts)

    def half_at(by):
        crosses = row_at + by >= 32 if by > 0 else row_at + by < 0
        return jnp.where(crosses, fz, f)

    def dev(blk, col):
        return {"blk": blk, "feat": col}

    links = Links({
        "halo0": (halo0_s, halo0_r), "halo1": (halo1_s, halo1_r), "z": (z_s, z_r),
        "core": (core_s, core_r), "fwd": (fwd_s, fwd_r), "noise": (noise_s, noise_r),
        "sq": (sq_s, sq_r), "sc": (sc_s, sc_r), "swap": (swap_s, swap_r),
    })
    go, arrive = links.go, links.arrive
    outs = []

    loads = [
        pltpu.make_async_copy(feat, win0.at[pl.ds(16, 8)], local.at[0]),
        pltpu.make_async_copy(mask, masks_in, local.at[1]),
        pltpu.make_async_copy(noise.at[0], noises.at[2], local.at[2]),
        pltpu.make_async_copy(noise.at[1], noises.at[zh], local.at[3]),
        pltpu.make_async_copy(weight, weights, local.at[4]),
    ]
    loaded = set()
    for copy in loads:
        copy.start()

    def load(i):
        loads[i].wait()
        loaded.add(i)

    def finish():
        links.finish()
        for i in range(5):
            if i not in loaded:
                loads[i].wait()
        for copy in outs:
            copy.wait()

    barrier = pltpu.get_barrier_semaphore()
    met = [dev(at(by), col) for by in (1, -1, 2, -2, 4, -4) for col in (f, fz)] + [dev(b, fz), dev(b, fc)]
    for device in met:
        pl.semaphore_signal(barrier, inc=1, device_id=device, device_id_type=MESH)

    ones = jnp.ones((8, TILE), F32)
    for t in range(TILES):
        wide = feat[t].astype(F32)
        row = lax.dot_general(
            ones, wide * wide, (((1,), (1,)), ((), ())),
            precision=lax.Precision.HIGHEST, preferred_element_type=F32,
        )
        squares[0, t : t + 1, :] = row[0:1, :]
    load(1)

    def take_mask(k, carry):
        masks[k] = masks_in[info[k]].astype(F32).astype(BF16)
        return carry

    lax.fori_loop(0, K, take_mask, 0)
    pl.semaphore_wait(barrier, len(met))

    class Halo:
        def __init__(self, name, WINDOW, count, size, half):
            self.name, self.window, self.count, self.size, self.half = name, WINDOW, count, size, half

        def part(self, block, q):
            return self.window.at[pl.ds(block + q * self.size, self.size)]

        def go(self, kind, q, src, slot, by, when=None):
            lands = {8: 0, 24: 1, 0: 2, 32: 3}[slot]
            go(
                self.name, kind * self.count + q, src, self.part(slot, q), dev(at(by), self.half(by)),
                lands * self.count + q, when,
            )

        def own(self, q, src=None, part=2):
            src = self.part(16, q) if src is None else src
            if part in (0, 2):
                self.go(2, q, src, 0, 2, low)
                self.go(3, q, src, 32, -2, high)
            if part in (1, 2):
                self.go(0, q, src, 8, 1)
                self.go(1, q, src, 24, -1)

        def far(self, q):
            @pl.when(low)
            def _():
                arrive(self.name, 3 * self.count + q)

            self.go(4, q, self.part(32, q), 0, 4, low)

            @pl.when(high)
            def _():
                arrive(self.name, 2 * self.count + q)

            self.go(5, q, self.part(0, q), 32, -4, high)

        def last(self, q):
            arrive(self.name, q)
            arrive(self.name, self.count + q)

            @pl.when(low)
            def _():
                arrive(self.name, 2 * self.count + q)

            @pl.when(high)
            def _():
                arrive(self.name, 3 * self.count + q)

    raw = Halo("halo0", win0, Q, QB, lambda by: f)
    clipped = Halo("halo1", win1, TILES, 1, half_at)
    go("sq", 0, squares.at[0], squares.at[1], dev(b, fc))
    for q in range(Q):
        raw.own(q, feat.at[pl.ds(q * QB, QB)], 0 if True else 2)
    arrive("sq", 0)
    mine_now = pl.ds(16, 8)
    chips[zh, mine_now, :] = squares[0] + squares[1]
    for i, by in enumerate((0, 1, -1, 2, -2)):
        there = pl.ds(16 - 8 * by, 8)
        go("sc", 2 * i, chips.at[zh, mine_now], chips.at[zh, there], dev(at(by), fz))
        if by:
            go("sc", 2 * i + 1, chips.at[zh, mine_now], chips.at[zh, there], dev(at(by), f))

    for q in range(Q):
        if True:
            raw.own(q, feat.at[pl.ds(q * QB, QB)], 1)

    def send_noise(t):
        go("noise", t, noise.at[1, t], noises.at[zh, t], dev(b, fz))

    for t in range(EARLY):
        send_noise(t)

    for q in range(Q):
        raw.far(q)
    load(0)
    for i in range(10):
        if i != 1:
            arrive("sc", i)
    scales[...] = 1.0 / jnp.maximum(1.0, jnp.sqrt(chips[0] + chips[1]))
    for q in range(Q):
        raw.last(q)

    def add_up(width, left, right):
        def step(i, acc):
            for u in range(4):
                k = i * 4 + u
                keep = info[KEEP + k].astype(F32)
                acc = acc * keep + jnp.dot(left(k), right(k), preferred_element_type=F32)
                sums[k, :, 0:width] = acc
            return acc

        lax.fori_loop(0, K // 4, step, jnp.zeros((TILE, width), F32))

    def scaled_mask(k):
        row = scales[pl.ds(info[SRC + k], 1), :]
        return (masks[k].astype(F32) * row).astype(BF16)

    add_up(TILE, scaled_mask, lambda k: win0[info[SRC + k]])

    load(2)

    def send_z(t):
        go("z", t, noisy.at[f, t], noisy.at[f, t], dev(b, fz))

    for t in range(TILES):
        has = info[HAS + t].astype(F32)
        rows = sums[info[LAST + t], :, 0:TILE] * has
        noisy[f, t] = (rows + noises[2, t].astype(F32)).astype(BF16)
        if t < WINDOW:
            send_z(t)
        go("core", t, noisy.at[f, t], noisy.at[f, t], dev(b, fc))

    load(4)

    def encode(t):
        arrive("core", t)
        arrive("fwd", t)
        left = jnp.concatenate([noisy[g, t] for g in range(4)], axis=1)
        rounded = jnp.dot(left, weights[0], preferred_element_type=F32).astype(BF16)
        wide = rounded.astype(F32)
        norm = jnp.sqrt(jnp.sum(wide * wide, axis=1, keepdims=True))
        inverse = 1.0 / jnp.maximum(1.0, norm)
        for g in range(4):
            encoded[g] = rounded[:, g * TILE : (g + 1) * TILE]
        own_one[t] = encoded[f]
        for half in range(2):
            win1[16 + t, half] = (encoded[half * 2 + core].astype(F32) * inverse).astype(BF16)
        clipped.own(t)
        copy = pltpu.make_async_copy(own_one.at[t], out_one.at[t], out_sem.at[t])
        copy.start()
        outs.append(copy)

    for t in range(TILES + LAG + 1):
        if t < TILES:
            if True and t + WINDOW < TILES:
                links.sent("z", t)
                send_z(t + WINDOW)
            arrive("z", t)
            if not True and t + WINDOW < TILES:
                send_z(t + WINDOW)
            go("fwd", t, noisy.at[fz, t], noisy.at[fz, t], dev(b, fc))
        if 0 <= t - 1 < TILES:
            encode(t - 1)
        if t >= LATE_AT:
            for late in range(EARLY + (t - LATE_AT) * DRIP, min(TILES, EARLY + (t - LATE_AT + 1) * DRIP)):
                send_noise(late)
        if 0 <= t - LAG - 1 < TILES:
            clipped.far(t - LAG - 1)

    for t in range(TILES):
        clipped.last(t)

    add_up(
        2 * TILE,
        lambda k: masks[k],
        lambda k: jnp.concatenate([win1[info[SRC + k], 0], win1[info[SRC + k], 1]], axis=1),
    )

    load(3)
    for t in range(TILES):
        arrive("noise", t)
        has = info[HAS + t].astype(F32)
        rows = sums[info[LAST + t]] * has
        for half in range(2):
            noisy_two[t, half] = (
                rows[:, half * TILE : (half + 1) * TILE] + noises[half, t].astype(F32)
            ).astype(BF16)
        go("swap", t, noisy_two.at[t], others.at[t], dev(b, fc))

    mine = pl.ds(pl.multiple_of(f * TILE, TILE), TILE)
    upper = pl.multiple_of(core * TILE, TILE)
    other = pl.multiple_of(TILE - core * TILE, TILE)
    for t in range(TILES):
        arrive("swap", t)
        left = jnp.concatenate(
            [noisy_two[t, 0], noisy_two[t, 1], others[t, 0], others[t, 1]], axis=1
        )
        right = jnp.concatenate(
            [weights[1, pl.ds(row, TILE), mine] for row in (upper, upper + 2 * TILE, other, other + 2 * TILE)],
            axis=0,
        )
        own_two[t] = jnp.dot(left, right, preferred_element_type=F32).astype(BF16)
        copy = pltpu.make_async_copy(own_two.at[t], out_two.at[t], out_sem.at[TILES + t])
        copy.start()
        outs.append(copy)
    finish()


def list_order(targets, sources, count):
    spots = jnp.arange(K)
    live = spots < count
    key = jnp.where(live, targets, TILES) * 64 + spots
    rank = jnp.sum(key[None, :] < key[:, None], axis=1)
    at = rank[:, None] == spots[None, :]
    perm = jnp.sum(jnp.where(at, spots[:, None], 0), axis=0)
    src = jnp.sum(jnp.where(at, sources[:, None], 0), axis=0)
    low = jnp.sum(jnp.where(at, (key // 64)[:, None], 0), axis=0)
    keep = (jnp.concatenate([jnp.full((1,), -1, low.dtype), low[:-1]]) == low).astype(jnp.int32)
    tiles = jnp.arange(TILES)
    last = jnp.maximum(jnp.sum(key[None, :] < (tiles[:, None] + 1) * 64, axis=1) - 1, 0)
    has = jnp.any((key // 64)[None, :] == tiles[:, None], axis=1)
    return jnp.concatenate([v.astype(jnp.int32) for v in (perm, src, keep, last, has)])


def per_device(
    features, hop_noise, encoder_weight, block_target, block_source, block_count, tile_mask
):
    info = list_order(block_target[0], block_source[0], block_count[0])
    tiles = (TILES, TILE, TILE)
    dma = pltpu.SemaphoreType.DMA
    anywhere = pl.BlockSpec(memory_space=pl.ANY)
    one, two = pl.pallas_call(
        kernel,
        out_shape=[jax.ShapeDtypeStruct(tiles, BF16)] * 2,
        in_specs=[
            pl.BlockSpec(memory_space=pltpu.SMEM),
            pl.BlockSpec(memory_space=pltpu.VMEM),
            anywhere, anywhere, anywhere,
        ],
        out_specs=[anywhere, anywhere],
        scratch_shapes=[
            pltpu.VMEM((K, TILE, TILE), BF16),
            pltpu.VMEM((K, 2, TILE, TILE), BF16),
            pltpu.VMEM((K, TILE, TILE), jnp.int32),
            pltpu.VMEM((K, TILE, TILE), BF16),
            pltpu.VMEM((2, 512, 512), BF16),
            pltpu.VMEM((3,) + tiles, BF16),
            pltpu.VMEM((4,) + tiles, BF16),
            pltpu.VMEM((K, TILE, 2 * TILE), F32),
            pltpu.VMEM((2, TILES, TILE), F32),
            pltpu.VMEM((2, K, TILE), F32),
            pltpu.VMEM((K, TILE), F32),
            pltpu.VMEM((4, TILE, TILE), BF16),
            pltpu.VMEM(tiles, BF16),
            pltpu.VMEM(tiles, BF16),
            pltpu.VMEM((TILES, 2, TILE, TILE), BF16),
            pltpu.VMEM((TILES, 2, TILE, TILE), BF16),
            dma((6 * TILES,)), dma((4 * TILES,)),
            dma((6 * TILES,)), dma((4 * TILES,)),
            dma((TILES,)), dma((TILES,)),
            dma((TILES,)), dma((TILES,)),
            dma((TILES,)), dma((TILES,)),
            dma((TILES,)), dma((TILES,)),
            dma((1,)), dma((1,)),
            dma((10,)), dma((10,)),
            dma((TILES,)), dma((TILES,)),
            dma((5,)),
            dma((2 * TILES,)),
        ],
        compiler_params=pltpu.CompilerParams(
            collective_id=0, has_side_effects=True, vmem_limit_bytes=60 << 20
        ),
    )(
        info,
        features.reshape(tiles),
        hop_noise.reshape((2,) + tiles),
        encoder_weight,
        tile_mask[0],
    )
    return one.reshape(features.shape), two.reshape(features.shape)


def solution(mesh):
    in_specs = (
        P("blk", "feat"),
        P(None, "blk", "feat"),
        P(),
        P("blk", None),
        P("blk", None),
        P("blk"),
        P("blk", None, None, None),
    )
    out_specs = (P("blk", "feat"), P("blk", "feat"))
    return jax.shard_map(
        per_device, mesh=mesh, in_specs=in_specs, out_specs=out_specs, check_vma=False
    )
```

time: 129 us -> 116 us (0.90)
  Pallas kernels: 119 us -> 107 us
  local copies, waits for them, and re-layouts: 6.44 us -> 3.99 us
    pallas_call x1, Pallas kernels: 119 us -> 107 us  [per_device(): pl.pallas_call(kernel, out_shape=[jax.ShapeDtypeStruct(tiles, BF16)] * 2,...]
    unnamed x10 -> x2, local copies, waits for them, and re-layouts: 6.36 us -> 3.34 us
where the time goes in v2:
time: 116 us; the launch traced here: 115 us
  Pallas kernels  107 us (92%)
  local copies, waits for them, and re-layouts  3.99 us (3%)
  other arithmetic  2.66 us (2%)
  between operations  1.31 us (1%)
    pallas_call x1, Pallas kernels, per_device(): pl.pallas_call(kernel, out_shape=[jax.ShapeDtypeStruct(tiles, BF16)] * 2,...  107 us
    unnamed x2, local copies, waits for them, and re-layouts  3.34 us

profile of v2, /device:TPU:1, one launch (start us, length us, event | category | flops | bytes accessed | tf_op | source)
XLA Modules:
  0.0 115.4 jit_solution(752489689690869516)
XLA Ops:
  1.3 0.7 and_select_fusion.1
  2.0 0.7 fusion.5
  2.6 0.2 convert_reduce_fusion.1
  2.8 0.2 convert_reduce_fusion
  3.0 0.1 fusion
  3.1 0.8 select_reduce_fusion
  3.9 0.1 compare_convert_fusion
  4.0 0.6 concatenate.7.info
  4.6 107.4 %shard_map.86 = (bf16[8,128,128]{2,1,0:T(8,128)(2,1)}, bf16[8,128,128]{2,1,0:T(8,128)(2,1)}) custom-call(s32[136]{0:T(256)} %concatenate.7.info, bf16[8,128,128]{2,1,0:T(8,128)(2,1)} %bitcast.18, bf16[2,8,128,128]{3,2,1,0:T(8,128)(2,1)} %bitcast.17, bf16[2,512,512]{2,1,0:T(8,128)(2,1)} %weight.1, s32[40,128,128]{2,1,0:T(8,128)} %bitcast.16), custom_call_target="tpu_custom_call" | custom-call | tf_op jit(solution)/shard_map/pallas_call | solution.py:361
  112.0 1.7 %copy.12 = bf16[1024,128]{1,0:T(8,128)(2,1)} copy(bf16[1024,128]{1,0:T(8,128)(2,1)} %bitcast.20) | data formatting | bytes 524288
  113.7 1.7 %copy.13 = bf16[1024,128]{1,0:T(8,128)(2,1)} copy(bf16[1024,128]{1,0:T(8,128)(2,1)} %bitcast.19) | data formatting | bytes 524288
  (3 shorter events, 0.0 us)

commit v3 on v2

--- a/solution.py
+++ b/solution.py
@@ -14,11 +14,12 @@
 LATE_AT = 7
 WINDOW = 3
 DRIP = 8
+MID = 0
 LAG = 2
 MESH = pl.DeviceIdType.MESH
 F32 = jnp.float32
 BF16 = jnp.bfloat16
-SRC, KEEP, LAST, HAS = 40, 80, 120, 128
+PERM, SRC, KEEP, LAST, HAS = range(5)
 
 
 class Links:
@@ -64,10 +65,33 @@
                 copy.wait_recv()
 
 
+def list_order(targets, sources, count):
+    spot_of = lax.broadcasted_iota(jnp.int32, (K, TILE), 0)
+    lane = lax.broadcasted_iota(jnp.int32, (K, TILE), 1)
+    same = spot_of == lane
+    key = jnp.where(lane[:1] < count, targets, TILES) * 64 + lane[:1]
+
+    def down(row):
+        return jnp.sum(jnp.where(same, row, 0), axis=1, keepdims=True)
+
+    def across(values, there):
+        return jnp.sum(jnp.where(there, values, 0), axis=0, keepdims=True)
+
+    key_down, source_down, target_down = down(key), down(sources), down(jnp.where(lane[:1] < count, targets, TILES))
+    rank = jnp.sum(jnp.where((lane < K) & (key < key_down), 1, 0), axis=1, keepdims=True)
+    at = rank == lane
+    now = across(target_down, at)
+    before = across(target_down, rank == lane - 1)
+    keep = jnp.where((now == before) & (lane[:1] > 0), 1, 0)
+    last = jnp.maximum(across(1, key_down < (lane + 1) * 64) - 1, 0)
+    has = jnp.minimum(across(1, target_down == lane), 1)
+    return across(spot_of, at), across(source_down, at), keep, last, has
+
+
 def kernel(
-    info, feat, noise, weight, mask, out_one, out_two,
-    win0, win1, masks_in, masks, weights, noises, noisy, sums, squares, chips, scales,
-    encoded, own_one, own_two, noisy_two, others,
+    targets, sources, count, feat, noise, weight, mask, out_one, out_two,
+    info, order, win0, win1, masks_in, masks, weights, noises, noisy, sums, squares, chips, scales,
+    encoded, own_one, own_two, noisy_two, others, partial,
     halo0_s, halo0_r, halo1_s, halo1_r, z_s, z_r, core_s, core_r, fwd_s, fwd_r,
     noise_s, noise_r, sq_s, sq_r, sc_s, sc_r, swap_s, swap_r, local, out_sem,
 ):
@@ -138,10 +162,18 @@
             precision=lax.Precision.HIGHEST, preferred_element_type=F32,
         )
         squares[0, t : t + 1, :] = row[0:1, :]
+    order[...] = jnp.zeros((8, TILE), jnp.int32)
+    order[6:7, 0:K] = targets[...]
+    order[7:8, 0:K] = sources[...]
+    for i, row in enumerate(list_order(order[6:7, :], order[7:8, :], count[0])):
+        order[i : i + 1, :] = row
+    listed = pltpu.make_async_copy(order, info, local.at[5])
+    listed.start()
+    listed.wait()
     load(1)
 
     def take_mask(k, carry):
-        masks[k] = masks_in[info[k]].astype(F32).astype(BF16)
+        masks[k] = masks_in[info[PERM, k]].astype(F32).astype(BF16)
         return carry
 
     lax.fori_loop(0, K, take_mask, 0)
@@ -229,11 +261,14 @@
     for q in range(Q):
         raw.last(q)
 
+    for t in range(EARLY, EARLY + MID):
+        send_noise(t)
+
     def add_up(width, left, right):
         def step(i, acc):
             for u in range(4):
                 k = i * 4 + u
-                keep = info[KEEP + k].astype(F32)
+                keep = info[KEEP, k].astype(F32)
                 acc = acc * keep + jnp.dot(left(k), right(k), preferred_element_type=F32)
                 sums[k, :, 0:width] = acc
             return acc
@@ -241,10 +276,10 @@
         lax.fori_loop(0, K // 4, step, jnp.zeros((TILE, width), F32))
 
     def scaled_mask(k):
-        row = scales[pl.ds(info[SRC + k], 1), :]
+        row = scales[pl.ds(info[SRC, k], 1), :]
         return (masks[k].astype(F32) * row).astype(BF16)
 
-    add_up(TILE, scaled_mask, lambda k: win0[info[SRC + k]])
+    add_up(TILE, scaled_mask, lambda k: win0[info[SRC, k]])
 
     load(2)
 
@@ -252,8 +287,8 @@
         go("z", t, noisy.at[f, t], noisy.at[f, t], dev(b, fz))
 
     for t in range(TILES):
-        has = info[HAS + t].astype(F32)
-        rows = sums[info[LAST + t], :, 0:TILE] * has
+        has = info[HAS, t].astype(F32)
+        rows = sums[info[LAST, t], :, 0:TILE] * has
         noisy[f, t] = (rows + noises[2, t].astype(F32)).astype(BF16)
         if t < WINDOW:
             send_z(t)
@@ -291,7 +326,8 @@
         if 0 <= t - 1 < TILES:
             encode(t - 1)
         if t >= LATE_AT:
-            for late in range(EARLY + (t - LATE_AT) * DRIP, min(TILES, EARLY + (t - LATE_AT + 1) * DRIP)):
+            sent = EARLY + MID + (t - LATE_AT) * DRIP
+            for late in range(sent, min(TILES, sent + DRIP)):
                 send_noise(late)
         if 0 <= t - LAG - 1 < TILES:
             clipped.far(t - LAG - 1)
@@ -302,59 +338,44 @@
     add_up(
         2 * TILE,
         lambda k: masks[k],
-        lambda k: jnp.concatenate([win1[info[SRC + k], 0], win1[info[SRC + k], 1]], axis=1),
+        lambda k: jnp.concatenate([win1[info[SRC, k], 0], win1[info[SRC, k], 1]], axis=1),
     )
 
     load(3)
+    mine = pl.ds(pl.multiple_of(f * TILE, TILE), TILE)
+    upper = pl.multiple_of(core * TILE, TILE)
+    other = pl.multiple_of(TILE - core * TILE, TILE)
+
+    def columns_of(start):
+        return jnp.concatenate([weights[1, pl.ds(row, TILE), mine] for row in (start, start + 2 * TILE)], axis=0)
+
     for t in range(TILES):
         arrive("noise", t)
-        has = info[HAS + t].astype(F32)
-        rows = sums[info[LAST + t]] * has
+        has = info[HAS, t].astype(F32)
+        rows = sums[info[LAST, t]] * has
         for half in range(2):
             noisy_two[t, half] = (
                 rows[:, half * TILE : (half + 1) * TILE] + noises[half, t].astype(F32)
             ).astype(BF16)
         go("swap", t, noisy_two.at[t], others.at[t], dev(b, fc))
 
-    mine = pl.ds(pl.multiple_of(f * TILE, TILE), TILE)
-    upper = pl.multiple_of(core * TILE, TILE)
-    other = pl.multiple_of(TILE - core * TILE, TILE)
+    for t in range(TILES):
+        left = jnp.concatenate([noisy_two[t, 0], noisy_two[t, 1]], axis=1)
+        partial[t] = jnp.dot(left, columns_of(upper), preferred_element_type=F32)
     for t in range(TILES):
         arrive("swap", t)
-        left = jnp.concatenate(
-            [noisy_two[t, 0], noisy_two[t, 1], others[t, 0], others[t, 1]], axis=1
-        )
-        right = jnp.concatenate(
-            [weights[1, pl.ds(row, TILE), mine] for row in (upper, upper + 2 * TILE, other, other + 2 * TILE)],
-            axis=0,
-        )
-        own_two[t] = jnp.dot(left, right, preferred_element_type=F32).astype(BF16)
+        left = jnp.concatenate([others[t, 0], others[t, 1]], axis=1)
+        rest = jnp.dot(left, columns_of(other), preferred_element_type=F32)
+        own_two[t] = (partial[t] + rest).astype(BF16)
         copy = pltpu.make_async_copy(own_two.at[t], out_two.at[t], out_sem.at[TILES + t])
         copy.start()
         outs.append(copy)
     finish()
 
 
-def list_order(targets, sources, count):
-    spots = jnp.arange(K)
-    live = spots < count
-    key = jnp.where(live, targets, TILES) * 64 + spots
-    rank = jnp.sum(key[None, :] < key[:, None], axis=1)
-    at = rank[:, None] == spots[None, :]
-    perm = jnp.sum(jnp.where(at, spots[:, None], 0), axis=0)
-    src = jnp.sum(jnp.where(at, sources[:, None], 0), axis=0)
-    low = jnp.sum(jnp.where(at, (key // 64)[:, None], 0), axis=0)
-    keep = (jnp.concatenate([jnp.full((1,), -1, low.dtype), low[:-1]]) == low).astype(jnp.int32)
-    tiles = jnp.arange(TILES)
-    last = jnp.maximum(jnp.sum(key[None, :] < (tiles[:, None] + 1) * 64, axis=1) - 1, 0)
-    has = jnp.any((key // 64)[None, :] == tiles[:, None], axis=1)
-    return jnp.concatenate([v.astype(jnp.int32) for v in (perm, src, keep, last, has)])
-
-
 def per_device(
     features, hop_noise, encoder_weight, block_target, block_source, block_count, tile_mask
 ):
-    info = list_order(block_target[0], block_source[0], block_count[0])
     tiles = (TILES, TILE, TILE)
     dma = pltpu.SemaphoreType.DMA
     anywhere = pl.BlockSpec(memory_space=pl.ANY)
@@ -362,12 +383,16 @@
         kernel,
         out_shape=[jax.ShapeDtypeStruct(tiles, BF16)] * 2,
         in_specs=[
+            pl.BlockSpec(memory_space=pltpu.VMEM),
+            pl.BlockSpec(memory_space=pltpu.VMEM),
             pl.BlockSpec(memory_space=pltpu.SMEM),
             pl.BlockSpec(memory_space=pltpu.VMEM),
             anywhere, anywhere, anywhere,
         ],
         out_specs=[anywhere, anywhere],
         scratch_shapes=[
+            pltpu.SMEM((8, TILE), jnp.int32),
+            pltpu.VMEM((8, TILE), jnp.int32),
             pltpu.VMEM((K, TILE, TILE), BF16),
             pltpu.VMEM((K, 2, TILE, TILE), BF16),
             pltpu.VMEM((K, TILE, TILE), jnp.int32),
@@ -384,6 +409,7 @@
             pltpu.VMEM(tiles, BF16),
             pltpu.VMEM((TILES, 2, TILE, TILE), BF16),
             pltpu.VMEM((TILES, 2, TILE, TILE), BF16),
+            pltpu.VMEM(tiles, F32),
             dma((6 * TILES,)), dma((4 * TILES,)),
             dma((6 * TILES,)), dma((4 * TILES,)),
             dma((TILES,)), dma((TILES,)),
@@ -393,14 +419,16 @@
             dma((1,)), dma((1,)),
             dma((10,)), dma((10,)),
             dma((TILES,)), dma((TILES,)),
-            dma((5,)),
+            dma((6,)),
             dma((2 * TILES,)),
         ],
         compiler_params=pltpu.CompilerParams(
-            collective_id=0, has_side_effects=True, vmem_limit_bytes=60 << 20
+            collective_id=0, has_side_effects=True, vmem_limit_bytes=(53 << 20) + (256 << 10)
         ),
     )(
-        info,
+        block_target,
+        block_source,
+        block_count,
         features.reshape(tiles),
         hop_noise.reshape((2,) + tiles),
         encoder_weight,

time: 116 us -> 111 us (0.957)
  other arithmetic: 2.66 us -> 0 us
  local copies, waits for them, and re-layouts: 3.99 us -> 2.71 us
    unnamed x2 -> x6, local copies, waits for them, and re-layouts: 3.34 us -> 2.71 us
where the time goes in v3:
time: 111 us
  Pallas kernels  107 us (96%)
  local copies, waits for them, and re-layouts  2.71 us (2%)
  between operations  1.3 us (1%)
    pallas_call x1, Pallas kernels, per_device(): pl.pallas_call(kernel, out_shape=[jax.ShapeDtypeStruct(tiles, BF16)] * 2,...  107 us
    unnamed x6, local copies, waits for them, and re-layouts  2.71 us

profile of v3, /device:TPU:1, one launch (start us, length us, event | category | flops | bytes accessed | tf_op | source)
XLA Modules:
  0.0 111.1 jit_solution(8136610719944473928)
XLA Ops:
  1.3 0.0 copy-start
  1.3 0.6 copy-done
  1.9 0.0 copy-start.1
  1.9 0.7 copy-done.1
  2.6 107.1 %shard_map.86 = (bf16[8,128,128]{2,1,0:T(8,128)(2,1)S(1)}, bf16[8,128,128]{2,1,0:T(8,128)(2,1)S(1)}) custom-call(s32[1,40]{1,0:T(1,128)S(1)} %copy-done, s32[1,40]{1,0:T(1,128)S(1)} %copy-done.1, s32[1]{0:T(128)S(6)} %copy.11.count, bf16[8,128,128]{2,1,0:T(8,128)(2,1)} %bitcast.9, bf16[2,8,128,128]{3,2,1,0:T(8,128)(2,1)} %bitcast.8, ...), custom_call_target="tpu_custom_call" | custom-call | tf_op jit(solution)/shard_map/pallas_call | solution.py:382
  109.7 0.7 copy.12
  110.4 0.7 copy.13
Async XLA Ops:
  1.3 0.7 copy-start
  1.9 0.7 copy-start.1

commit v4 on v3

--- a/solution.py
+++ b/solution.py
@@ -105,7 +105,6 @@
     fd = lax.rem(fc + 2, 4)
     row_at = lax.rem(b, 32)
     x = lax.rem(b, 4)
-    inner = (x == 1) | (x == 2)
     low, high = x < 2, x >= 2
 
     def at(by):
@@ -150,7 +149,7 @@
             copy.wait()
 
     barrier = pltpu.get_barrier_semaphore()
-    met = [dev(at(by), col) for by in (1, -1, 2, -2, 4, -4) for col in (f, fz)] + [dev(b, fz), dev(b, fc)]
+    met = [dev(at(by), col) for by in (1, -1, 2, -2, 3, -3) for col in (f, fz)] + [dev(b, fz), dev(b, fc)]
     for device in met:
         pl.semaphore_signal(barrier, inc=1, device_id=device, device_id_type=MESH)
 
@@ -193,45 +192,34 @@
                 lands * self.count + q, when,
             )
 
-        def own(self, q, src=None, part=2):
+        def own(self, q, src=None):
             src = self.part(16, q) if src is None else src
-            if part in (0, 2):
-                self.go(2, q, src, 0, 2, low)
-                self.go(3, q, src, 32, -2, high)
-            if part in (1, 2):
-                self.go(0, q, src, 8, 1)
-                self.go(1, q, src, 24, -1)
+            self.go(0, q, src, 8, 1)
+            self.go(1, q, src, 24, -1)
 
         def far(self, q):
-            @pl.when(low)
-            def _():
-                arrive(self.name, 3 * self.count + q)
-
-            self.go(4, q, self.part(32, q), 0, 4, low)
-
-            @pl.when(high)
-            def _():
-                arrive(self.name, 2 * self.count + q)
-
-            self.go(5, q, self.part(0, q), 32, -4, high)
+            for kind, (below, above) in enumerate(((3, -3), (1, -1))):
+                @pl.when(low)
+                def _():
+                    arrive(self.name, (1 - kind) * self.count + q)
+
+                self.go(2 + kind, q, self.part((24, 8)[kind], q), 0, below, low)
+
+                @pl.when(high)
+                def _():
+                    arrive(self.name, kind * self.count + q)
+
+                self.go(4 + kind, q, self.part((8, 24)[kind], q), 32, above, high)
 
         def last(self, q):
-            arrive(self.name, q)
-            arrive(self.name, self.count + q)
-
-            @pl.when(low)
-            def _():
-                arrive(self.name, 2 * self.count + q)
-
-            @pl.when(high)
-            def _():
-                arrive(self.name, 3 * self.count + q)
+            arrive(self.name, 2 * self.count + q)
+            arrive(self.name, 3 * self.count + q)
 
     raw = Halo("halo0", win0, Q, QB, lambda by: f)
     clipped = Halo("halo1", win1, TILES, 1, half_at)
     go("sq", 0, squares.at[0], squares.at[1], dev(b, fc))
     for q in range(Q):
-        raw.own(q, feat.at[pl.ds(q * QB, QB)], 0 if True else 2)
+        raw.own(q, feat.at[pl.ds(q * QB, QB)])
     arrive("sq", 0)
     mine_now = pl.ds(16, 8)
     chips[zh, mine_now, :] = squares[0] + squares[1]
@@ -240,10 +228,6 @@
         go("sc", 2 * i, chips.at[zh, mine_now], chips.at[zh, there], dev(at(by), fz))
         if by:
             go("sc", 2 * i + 1, chips.at[zh, mine_now], chips.at[zh, there], dev(at(by), f))
-
-    for q in range(Q):
-        if True:
-            raw.own(q, feat.at[pl.ds(q * QB, QB)], 1)
 
     def send_noise(t):
         go("noise", t, noise.at[1, t], noises.at[zh, t], dev(b, fz))

time: 111 us -> 110 us (level)
    pallas_call x1, Pallas kernels: 107 us -> 106 us  [per_device(): pl.pallas_call(kernel, out_shape=[jax.ShapeDtypeStruct(tiles, BF16)] * 2,...]
where the time goes in v4:
time: 110 us
  Pallas kernels  106 us (96%)
  local copies, waits for them, and re-layouts  2.71 us (2%)
  between operations  1.3 us (1%)
    pallas_call x1, Pallas kernels, per_device(): pl.pallas_call(kernel, out_shape=[jax.ShapeDtypeStruct(tiles, BF16)] * 2,...  106 us
    unnamed x6, local copies, waits for them, and re-layouts  2.71 us

profile of v4, /device:TPU:1, one launch (start us, length us, event | category | flops | bytes accessed | tf_op | source)
XLA Modules:
  0.0 109.9 jit_solution(12667189904581723595)
XLA Ops:
  1.3 0.0 copy-start
  1.3 0.6 copy-done
  1.9 0.0 copy-start.1
  1.9 0.7 copy-done.1
  2.6 105.9 %shard_map.86 = (bf16[8,128,128]{2,1,0:T(8,128)(2,1)S(1)}, bf16[8,128,128]{2,1,0:T(8,128)(2,1)S(1)}) custom-call(s32[1,40]{1,0:T(1,128)S(1)} %copy-done, s32[1,40]{1,0:T(1,128)S(1)} %copy-done.1, s32[1]{0:T(128)S(6)} %copy.11.count, bf16[8,128,128]{2,1,0:T(8,128)(2,1)} %bitcast.9, bf16[2,8,128,128]{3,2,1,0:T(8,128)(2,1)} %bitcast.8, ...), custom_call_target="tpu_custom_call" | custom-call | tf_op jit(solution)/shard_map/pallas_call | solution.py:366
  108.5 0.7 copy.12
  109.2 0.7 copy.13
Async XLA Ops:
  1.3 0.7 copy-start
  1.9 0.7 copy-start.1

commit v5 on v4

--- a/solution.py
+++ b/solution.py
@@ -12,10 +12,11 @@
 QB = TILES // Q
 EARLY = 3
 LATE_AT = 7
-WINDOW = 3
+WINDOW = 4
 DRIP = 8
 MID = 0
-LAG = 2
+UNROLL = 10
+LAG = 3
 MESH = pl.DeviceIdType.MESH
 F32 = jnp.float32
 BF16 = jnp.bfloat16
@@ -161,10 +162,13 @@
             precision=lax.Precision.HIGHEST, preferred_element_type=F32,
         )
         squares[0, t : t + 1, :] = row[0:1, :]
+    lanes = lax.broadcasted_iota(jnp.int32, (1, TILE), 1)
+    target_row = source_row = jnp.zeros((1, TILE), jnp.int32)
+    for k in range(K):
+        target_row = jnp.where(lanes == k, targets[k], target_row)
+        source_row = jnp.where(lanes == k, sources[k], source_row)
     order[...] = jnp.zeros((8, TILE), jnp.int32)
-    order[6:7, 0:K] = targets[...]
-    order[7:8, 0:K] = sources[...]
-    for i, row in enumerate(list_order(order[6:7, :], order[7:8, :], count[0])):
+    for i, row in enumerate(list_order(target_row, source_row, count[0])):
         order[i : i + 1, :] = row
     listed = pltpu.make_async_copy(order, info, local.at[5])
     listed.start()
@@ -250,14 +254,14 @@
 
     def add_up(width, left, right):
         def step(i, acc):
-            for u in range(4):
-                k = i * 4 + u
+            for u in range(UNROLL):
+                k = i * UNROLL + u
                 keep = info[KEEP, k].astype(F32)
                 acc = acc * keep + jnp.dot(left(k), right(k), preferred_element_type=F32)
                 sums[k, :, 0:width] = acc
             return acc
 
-        lax.fori_loop(0, K // 4, step, jnp.zeros((TILE, width), F32))
+        lax.fori_loop(0, K // UNROLL, step, jnp.zeros((TILE, width), F32))
 
     def scaled_mask(k):
         row = scales[pl.ds(info[SRC, k], 1), :]
@@ -300,12 +304,10 @@
 
     for t in range(TILES + LAG + 1):
         if t < TILES:
-            if True and t + WINDOW < TILES:
+            if t + WINDOW < TILES:
                 links.sent("z", t)
                 send_z(t + WINDOW)
             arrive("z", t)
-            if not True and t + WINDOW < TILES:
-                send_z(t + WINDOW)
             go("fwd", t, noisy.at[fz, t], noisy.at[fz, t], dev(b, fc))
         if 0 <= t - 1 < TILES:
             encode(t - 1)
@@ -367,8 +369,8 @@
         kernel,
         out_shape=[jax.ShapeDtypeStruct(tiles, BF16)] * 2,
         in_specs=[
-            pl.BlockSpec(memory_space=pltpu.VMEM),
-            pl.BlockSpec(memory_space=pltpu.VMEM),
+            pl.BlockSpec(memory_space=pltpu.SMEM),
+            pl.BlockSpec(memory_space=pltpu.SMEM),
             pl.BlockSpec(memory_space=pltpu.SMEM),
             pl.BlockSpec(memory_space=pltpu.VMEM),
             anywhere, anywhere, anywhere,
@@ -410,8 +412,8 @@
             collective_id=0, has_side_effects=True, vmem_limit_bytes=(53 << 20) + (256 << 10)
         ),
     )(
-        block_target,
-        block_source,
+        block_target.reshape(K),
+        block_source.reshape(K),
         block_count,
         features.reshape(tiles),
         hop_noise.reshape((2,) + tiles),

time: 110 us -> 109 us (level)
  Pallas kernels: 106 us -> 104 us
    pallas_call x1, Pallas kernels: 106 us -> 104 us  [per_device(): pl.pallas_call(kernel, out_shape=[jax.ShapeDtypeStruct(tiles, BF16)] * 2,...]
where the time goes in v5:
time: 109 us; the launch traced here: 108 us
  Pallas kernels  104 us (95%)
  local copies, waits for them, and re-layouts  2.71 us (2%)
  between operations  1.3 us (1%)
    pallas_call x1, Pallas kernels, per_device(): pl.pallas_call(kernel, out_shape=[jax.ShapeDtypeStruct(tiles, BF16)] * 2,...  104 us
    unnamed x6, local copies, waits for them, and re-layouts  2.71 us

profile of v5, /device:TPU:1, one launch (start us, length us, event | category | flops | bytes accessed | tf_op | source)
XLA Modules:
  0.0 108.0 jit_solution(15376734030184437696)
XLA Ops:
  1.3 0.0 copy-start
  1.3 0.6 copy-done
  1.9 0.0 copy-start.1
  1.9 0.7 copy-done.1
  2.6 103.9 %shard_map.86 = (bf16[8,128,128]{2,1,0:T(8,128)(2,1)S(1)}, bf16[8,128,128]{2,1,0:T(8,128)(2,1)S(1)}) custom-call(s32[40]{0:T(128)S(1)} %bitcast.9, s32[40]{0:T(128)S(1)} %bitcast.10, s32[1]{0:T(128)S(6)} %copy.11.count, bf16[8,128,128]{2,1,0:T(8,128)(2,1)} %bitcast.13, bf16[2,8,128,128]{3,2,1,0:T(8,128)(2,1)} %bitcast.12, bf16[2,512,512]{2,1,0:T(8,128)(2,1)} %weight.1, ...), custom_call_target="tpu_custom_call" | custom-call | tf_op jit(solution)/shard_map/pallas_call | solution.py:368
  106.5 0.7 copy.12
  107.2 0.7 copy.13
Async XLA Ops:
  1.3 0.7 copy-start
  1.9 0.7 copy-start.1

commit v6 on v5

--- a/solution.py
+++ b/solution.py
@@ -13,9 +13,10 @@
 EARLY = 3
 LATE_AT = 7
 WINDOW = 4
-DRIP = 8
+DRIP = 2
 MID = 0
 UNROLL = 10
+ELAG = 1
 LAG = 3
 MESH = pl.DeviceIdType.MESH
 F32 = jnp.float32
@@ -90,7 +91,7 @@
 
 
 def kernel(
-    targets, sources, count, feat, noise, weight, mask, out_one, out_two,
+    lists, feat, noise, weight, mask, out_one, out_two,
     info, order, win0, win1, masks_in, masks, weights, noises, noisy, sums, squares, chips, scales,
     encoded, own_one, own_two, noisy_two, others, partial,
     halo0_s, halo0_r, halo1_s, halo1_r, z_s, z_r, core_s, core_r, fwd_s, fwd_r,
@@ -165,10 +166,10 @@
     lanes = lax.broadcasted_iota(jnp.int32, (1, TILE), 1)
     target_row = source_row = jnp.zeros((1, TILE), jnp.int32)
     for k in range(K):
-        target_row = jnp.where(lanes == k, targets[k], target_row)
-        source_row = jnp.where(lanes == k, sources[k], source_row)
+        target_row = jnp.where(lanes == k, lists[k], target_row)
+        source_row = jnp.where(lanes == k, lists[K + k], source_row)
     order[...] = jnp.zeros((8, TILE), jnp.int32)
-    for i, row in enumerate(list_order(target_row, source_row, count[0])):
+    for i, row in enumerate(list_order(target_row, source_row, lists[2 * K])):
         order[i : i + 1, :] = row
     listed = pltpu.make_async_copy(order, info, local.at[5])
     listed.start()
@@ -302,21 +303,21 @@
         copy.start()
         outs.append(copy)
 
-    for t in range(TILES + LAG + 1):
+    for t in range(TILES + LAG + ELAG):
         if t < TILES:
             if t + WINDOW < TILES:
                 links.sent("z", t)
                 send_z(t + WINDOW)
             arrive("z", t)
             go("fwd", t, noisy.at[fz, t], noisy.at[fz, t], dev(b, fc))
-        if 0 <= t - 1 < TILES:
-            encode(t - 1)
+        if 0 <= t - ELAG < TILES:
+            encode(t - ELAG)
         if t >= LATE_AT:
             sent = EARLY + MID + (t - LATE_AT) * DRIP
             for late in range(sent, min(TILES, sent + DRIP)):
                 send_noise(late)
-        if 0 <= t - LAG - 1 < TILES:
-            clipped.far(t - LAG - 1)
+        if 0 <= t - LAG - ELAG < TILES:
+            clipped.far(t - LAG - ELAG)
 
     for t in range(TILES):
         clipped.last(t)
@@ -369,8 +370,6 @@
         kernel,
         out_shape=[jax.ShapeDtypeStruct(tiles, BF16)] * 2,
         in_specs=[
-            pl.BlockSpec(memory_space=pltpu.SMEM),
-            pl.BlockSpec(memory_space=pltpu.SMEM),
             pl.BlockSpec(memory_space=pltpu.SMEM),
             pl.BlockSpec(memory_space=pltpu.VMEM),
             anywhere, anywhere, anywhere,
@@ -412,9 +411,7 @@
             collective_id=0, has_side_effects=True, vmem_limit_bytes=(53 << 20) + (256 << 10)
         ),
     )(
-        block_target.reshape(K),
-        block_source.reshape(K),
-        block_count,
+        jnp.concatenate([block_target[0], block_source[0], block_count]),
         features.reshape(tiles),
         hop_noise.reshape((2,) + tiles),
         encoder_weight,

time: 109 us -> 108 us (level)
  local copies, waits for them, and re-layouts: 2.71 us -> 1.41 us
    unnamed x6 -> x2, local copies, waits for them, and re-layouts: 2.71 us -> 1.41 us
    pallas_call x1, Pallas kernels: 104 us -> 103 us  [per_device(): pl.pallas_call(kernel, out_shape=[jax.ShapeDtypeStruct(tiles, BF16)] * 2,...]
where the time goes in v6:
time: 108 us; the launch traced here: 106 us
  Pallas kernels  103 us (95%)
  local copies, waits for them, and re-layouts  1.41 us (1%)
  between operations  1.29 us (1%)
    pallas_call x1, Pallas kernels, per_device(): pl.pallas_call(kernel, out_shape=[jax.ShapeDtypeStruct(tiles, BF16)] * 2,...  103 us

profile of v6, /device:TPU:1, one launch (start us, length us, event | category | flops | bytes accessed | tf_op | source)
XLA Modules:
  0.0 106.1 jit_solution(11480264587062670200)
XLA Ops:
  1.3 0.7 pad_add_fusion.lists
  2.0 102.7 %shard_map.86 = (bf16[8,128,128]{2,1,0:T(8,128)(2,1)S(1)}, bf16[8,128,128]{2,1,0:T(8,128)(2,1)S(1)}) custom-call(s32[81]{0:T(128)S(1)} %pad_add_fusion.lists, bf16[8,128,128]{2,1,0:T(8,128)(2,1)} %bitcast.11, bf16[2,8,128,128]{3,2,1,0:T(8,128)(2,1)} %bitcast.10, bf16[2,512,512]{2,1,0:T(8,128)(2,1)} %weight.1, s32[40,128,128]{2,1,0:T(8,128)} %bitcast.9), custom_call_target="tpu_custom_call" | custom-call | tf_op jit(solution)/shard_map/pallas_call | solution.py:369
  104.7 0.7 copy.12
  105.4 0.7 copy.13

commit v7 on v6

--- a/solution.py
+++ b/solution.py
@@ -155,14 +155,9 @@
     for device in met:
         pl.semaphore_signal(barrier, inc=1, device_id=device, device_id_type=MESH)
 
-    ones = jnp.ones((8, TILE), F32)
     for t in range(TILES):
         wide = feat[t].astype(F32)
-        row = lax.dot_general(
-            ones, wide * wide, (((1,), (1,)), ((), ())),
-            precision=lax.Precision.HIGHEST, preferred_element_type=F32,
-        )
-        squares[0, t : t + 1, :] = row[0:1, :]
+        squares[0, t : t + 1, :] = jnp.sum((wide * wide).T, axis=0, keepdims=True)
     lanes = lax.broadcasted_iota(jnp.int32, (1, TILE), 1)
     target_row = source_row = jnp.zeros((1, TILE), jnp.int32)
     for k in range(K):

time: 108 us -> 108 us (level)
  no operation moved by 1% of the time
where the time goes in v7:
time: 108 us; the launch traced here: 106 us
  Pallas kernels  103 us (95%)
  local copies, waits for them, and re-layouts  1.41 us (1%)
  between operations  1.29 us (1%)
    pallas_call x1, Pallas kernels, per_device(): pl.pallas_call(kernel, out_shape=[jax.ShapeDtypeStruct(tiles, BF16)] * 2,...  103 us

profile of v7, /device:TPU:1, one launch (start us, length us, event | category | flops | bytes accessed | tf_op | source)
XLA Modules:
  0.0 106.0 jit_solution(9350585206976035942)
XLA Ops:
  1.3 0.7 pad_add_fusion.lists
  2.0 102.6 %shard_map.86 = (bf16[8,128,128]{2,1,0:T(8,128)(2,1)S(1)}, bf16[8,128,128]{2,1,0:T(8,128)(2,1)S(1)}) custom-call(s32[81]{0:T(128)S(1)} %pad_add_fusion.lists, bf16[8,128,128]{2,1,0:T(8,128)(2,1)} %bitcast.11, bf16[2,8,128,128]{3,2,1,0:T(8,128)(2,1)} %bitcast.10, bf16[2,512,512]{2,1,0:T(8,128)(2,1)} %weight.1, s32[40,128,128]{2,1,0:T(8,128)} %bitcast.9), custom_call_target="tpu_custom_call" | custom-call | tf_op jit(solution)/shard_map/pallas_call | solution.py:364
  104.6 0.7 copy.12
  105.3 0.7 copy.13
